TPU v7x, 32 devices: a whole 2x2x4 slice. The times are simulated.
32 devices in a mesh: groups: 2 (over y), row: 16 (over z, x, core).
Axes of the slice: x: 2, y: 2, z: 4, core: 2. Of those that a mesh axis runs over, the one named last changes fastest.
Arguments:
- object_tiles: bfloat16 [8192, 2, 2048], P(('groups', 'row')), parts along dimension 0, may hold values from -4 to 4
- probe: float32 [4, 256, 2, 256], replicated, may hold values from -3 to 3
- measured: bfloat16 [192, 256, 256], P(('groups', 'row')), parts along dimension 0, may hold values from 0.19921875 to 2.5
- offset_row: int32 [192], P(('groups', 'row')), parts along dimension 0, may hold values from 0 to 255
- offset_col: int32 [192], P(('groups', 'row')), parts along dimension 0, may hold values from 0 to 1791
- subpixel: int32 [192], P(('groups', 'row')), parts along dimension 0, may hold values from 0 to 15
- live_count: int32 [32], P(('groups', 'row')), parts along dimension 0, may hold values from 1 to 6, 48 in all
Outputs:
- object_grad: float32 [8192, 2, 2048], P(('groups', 'row')), parts along dimension 0
- probe_grad: float32 [8, 256, 2, 256], P('groups'), parts along dimension 0
- position_grad: float32 [2, 192], P(None, ('groups', 'row')), parts along dimension 1
There are 2 independent parts, one for each index of `groups`. A program takes and returns all parts, laid end to end along the dimension named above; an argument that names none is the same for every part. Nothing has to cross between parts.
Inputs may be any that keep to these rules, and one draw needn't show every extreme that they name: Device d's live slots are its first live_count[d] slots; live_count sums to 48 and reaches 6 on some device.
All inputs are finite; a program needn't handle non-finite values.
Results may differ from a plain program's by a relative error of at most 0.0099.
Values may be sent and summed in bfloat16 or wider, within the bound.
No kernel may reach another device: no remote copies, remote signals or barrier semaphores. Data moves between devices by JAX's collectives and lax.ppermute only.
A program may use at most 128 MiB of HBM per device.

v0:
```python
import math

import jax
import jax.numpy as jnp
from jax import lax
from jax.sharding import PartitionSpec as P


def passed_along(x, axis, by):
    length = lax.axis_size(axis)
    pairs = [(i, i + by) for i in range(length) if 0 <= i + by < length]
    return lax.ppermute(x, axis, pairs)


def dft_tables(patch):
    index = jnp.arange(patch, dtype=jnp.int32)
    phase = index[:, None] * index[None, :] % patch
    angle = phase.astype(jnp.float32) * (2.0 * math.pi / patch)
    scale = 1.0 / math.sqrt(patch)
    cosine = (jnp.cos(angle) * scale).astype(jnp.bfloat16)
    sine = (jnp.sin(angle) * scale).astype(jnp.bfloat16)
    along_x = jnp.concatenate(
        [jnp.concatenate([cosine, -sine], 1), jnp.concatenate([sine, cosine], 1)], 0
    )
    along_y = jnp.concatenate(
        [
            jnp.stack([cosine, sine], -1).reshape(patch, 2 * patch),
            jnp.stack([-sine, cosine], -1).reshape(patch, 2 * patch),
        ],
        0,
    )
    inverse_y = jnp.stack(
        [jnp.concatenate([cosine, -sine], 1), jnp.concatenate([sine, cosine], 1)], 1
    ).reshape(2 * patch, 2 * patch)
    inverse_x = jnp.concatenate(
        [jnp.concatenate([cosine, sine], 1), jnp.concatenate([-sine, cosine], 1)], 0
    )
    return (along_x, along_y, inverse_y, inverse_x)


def fractions(code):
    return ((code // 4).astype(jnp.float32) * 0.25, (code % 4).astype(jnp.float32) * 0.25)


def interpolate(window, code):
    frac_y, frac_x = fractions(code)
    cells = window.astype(jnp.float32)
    size = cells.shape[0] - 1
    upper = (1.0 - frac_x) * cells[:size, :, :size] + frac_x * cells[:size, :, 1:]
    lower = (1.0 - frac_x) * cells[1:, :, :size] + frac_x * cells[1:, :, 1:]
    return (1.0 - frac_y) * upper + frac_y * lower


def spread(grad_patch, frac_y, frac_x):

    def sideways(part):
        return jnp.pad((1.0 - frac_x) * part, ((0, 0), (0, 0), (0, 1))) + jnp.pad(
            frac_x * part, ((0, 0), (0, 0), (1, 0))
        )

    upper = sideways((1.0 - frac_y) * grad_patch)
    lower = sideways(frac_y * grad_patch)
    return jnp.pad(upper, ((0, 1), (0, 0), (0, 0))) + jnp.pad(lower, ((1, 0), (0, 0), (0, 0)))


def slopes(window, grad_patch, frac_y, frac_x):
    cells = window.astype(jnp.float32)
    size = cells.shape[0] - 1
    down = cells[1:] - cells[:size]
    slope_y = (1.0 - frac_x) * down[:, :, :size] + frac_x * down[:, :, 1:]
    across = cells[:, :, 1:] - cells[:, :, :size]
    slope_x = (1.0 - frac_y) * across[:size] + frac_y * across[1:]
    return (jnp.sum(grad_patch * slope_y) / size, jnp.sum(grad_patch * slope_x) / size)


def project(patch_obj, amplitude, probe, tables):
    along_x, along_y, inverse_y, inverse_x = tables
    modes = probe.shape[0]
    size = probe.shape[1]
    preal = probe[:, :, 0, :]
    pimag = probe[:, :, 1, :]
    oreal = patch_obj[:, 0, :]
    oimag = patch_obj[:, 1, :]
    wave = jnp.stack([preal * oreal - pimag * oimag, preal * oimag + pimag * oreal], axis=2).astype(
        jnp.bfloat16
    )
    first = jnp.dot(
        wave.reshape(modes * size, 2 * size), along_x, preferred_element_type=jnp.float32
    ).astype(jnp.bfloat16)
    far = jnp.einsum(
        "ab,mbk->mak",
        along_y,
        first.reshape(modes, 2 * size, size),
        preferred_element_type=jnp.float32,
    )
    far = far.reshape(modes, 2, size, size)
    modulus = jnp.maximum(jnp.sqrt(jnp.sum(far * far, axis=(0, 1))), 0.5)
    ratio = 1.0 - amplitude.astype(jnp.float32) / modulus
    error = (far * ratio).astype(jnp.bfloat16)
    back = jnp.einsum(
        "ab,mbk->mak",
        inverse_y,
        error.reshape(modes, 2 * size, size),
        preferred_element_type=jnp.float32,
    ).astype(jnp.bfloat16)
    exit_grad = jnp.dot(
        back.reshape(modes * size, 2 * size), inverse_x, preferred_element_type=jnp.float32
    ).reshape(modes, size, 2, size)
    ureal = exit_grad[:, :, 0, :]
    uimag = exit_grad[:, :, 1, :]
    obj_grad = jnp.stack(
        [jnp.sum(preal * ureal + pimag * uimag, 0), jnp.sum(preal * uimag - pimag * ureal, 0)],
        axis=1,
    )
    probe_term = jnp.stack([oreal * ureal + oimag * uimag, oreal * uimag - oimag * ureal], axis=2)
    return (obj_grad, probe_term)


def shards(object_tiles, probe, measured, offset_row, offset_col, subpixel, live_count):
    rows = object_tiles.shape[0]
    width = object_tiles.shape[2]
    size = probe.shape[1]
    slots = measured.shape[0]
    spare = slots // 2
    tables = dft_tables(size)
    count = live_count[0]
    slot_ids = jnp.arange(slots, dtype=jnp.int32)
    rim = passed_along(object_tiles, "row", -1)
    extended = jnp.concatenate([object_tiles, rim], axis=0)

    def cut(index):
        return lax.dynamic_slice(
            extended, (offset_row[index], 0, offset_col[index]), (size + 1, 2, size + 1)
        )

    windows = lax.map(cut, slot_ids)
    empty_grads = jnp.zeros((slots + spare, size, 2, size), jnp.float32)
    empty_probe = jnp.zeros(probe.shape, jnp.float32)

    def own_slot(index, carry):
        grads, probe_acc = carry
        patch_obj = interpolate(windows[index], subpixel[index])
        obj_grad, probe_term = project(patch_obj, measured[index], probe, tables)
        return (grads.at[index].set(obj_grad), probe_acc + probe_term)

    grads, probe_acc = lax.fori_loop(0, count, own_slot, (empty_grads, empty_probe))
    probe_grad = lax.psum(probe_acc, "row")

    def settle(index, carry):
        grad_ext, moved = carry
        frac_y, frac_x = fractions(subpixel[index])
        obj_grad = grads[index]
        corner = (offset_row[index], 0, offset_col[index])
        region = lax.dynamic_slice(grad_ext, corner, (size + 1, 2, size + 1))
        grad_ext = lax.dynamic_update_slice(
            grad_ext, region + spread(obj_grad, frac_y, frac_x), corner
        )
        slope_y, slope_x = slopes(windows[index], obj_grad, frac_y, frac_x)
        moved = moved.at[:, index].set(jnp.stack([slope_y, slope_x]))
        return (grad_ext, moved)

    start = (jnp.zeros((rows + size, 2, width), jnp.float32), jnp.zeros((2, slots), jnp.float32))
    grad_ext, moved = lax.fori_loop(0, count, settle, start)
    own_rows = grad_ext[:rows]
    below = passed_along(grad_ext[rows:], "row", 1)
    object_grad = own_rows.at[:size].add(below)
    return (object_grad, probe_grad, moved)


def solution(mesh):
    in_specs = (
        P(("groups", "row"), None, None),
        P(),
        P(("groups", "row"), None, None),
        P(("groups", "row")),
        P(("groups", "row")),
        P(("groups", "row")),
        P(("groups", "row")),
    )
    out_specs = (
        P(("groups", "row"), None, None),
        P("groups", None, None, None),
        P(None, ("groups", "row")),
    )
    return jax.shard_map(shards, mesh=mesh, in_specs=in_specs, out_specs=out_specs, check_vma=False)
```

profile of v0, /device:TPU:16, one launch (start us, length us, event | category | flops | bytes accessed | tf_op | source)
XLA Modules:
  0.0 836.7 jit_solution(12319592840080099803)
XLA Ops:
  7.2 2.7 collective-permute-start
  19.6 14.2 %collective-permute-done = bf16[256,2,2048]{2,1,0:T(2,128)(2,1)} collective-permute-done((bf16[256,2,2048]{2,1,0:T(2,128)(2,1)}, bf16[256,2,2048]{2,1,0:T(2,128)(2,1)}, u32[]{:S(2)}, u32[]{:S(2)}) %collective-permute-start) | collective-permute-done | bytes 2097184 | tf_op jit(solution)/shard_map/ppermute | solution.py:12
  33.8 9.6 %pad_maximum_fusion.1 = bf16[512,2,2048]{2,1,0:T(2,128)(2,1)} fusion(bf16[256,2,2048]{2,1,0:T(2,128)(2,1)} %collective-permute-done, bf16[256,2,2048]{2,1,0:T(2,128)(2,1)} %param.21), kind=kLoop, calls=%fused_computation.72 | loop fusion | flops 2097152 | bytes 8388608 | tf_op jit(solution)/shard_map/concatenate | solution.py:129
  43.4 56.7 %while.42 = (s32[]{:T(128)}, bf16[6,257,2,257]{3,2,1,0:T(2,128)(2,1)}, s32[6]{0:T(128)S(1)}, s32[6]{0:T(128)S(1)}, s32[6]{0:T(128)S(1)}, /*index=5*/bf16[512,2,2...) while((s32[]{:T(128)}, bf16[6,257,2,257]{3,2,1,0:T(2,128)(2,1)}, ...), condition=%wide.region_1.2_spmd, body=%wide.region_0.1_spmd.sunk | while | flops 11 | bytes 789771 | solution.py:136
  50.2 2.6 bitcast_dynamic-update-slice_fusion.2
  59.7 2.6 bitcast_dynamic-update-slice_fusion.2
  69.1 2.6 bitcast_dynamic-update-slice_fusion.2
  78.5 2.6 bitcast_dynamic-update-slice_fusion.2
  87.9 2.6 bitcast_dynamic-update-slice_fusion.2
  97.3 2.6 bitcast_dynamic-update-slice_fusion.2
  101.6 3.6 broadcast_in_dim.22
  105.2 64.7 %while.43 = (s32[]{:T(128)}, f32[9,256,2,256]{3,2,1,0:T(2,128)}, f32[4,256,2,256]{3,1,2,0:T(8,128)}, s32[]{:T(128)}, f32[4,256,2,256]{3,1,2,0:T(8,128)S(1)}, /*i...) while((s32[]{:T(128)}, f32[9,256,2,256]{3,2,1,0:T(2,128)}, ...), condition=%wide.region_8.9_spmd, body=%wide.region_2.8_spmd.sunk | while | flops 2159608832 | bytes 92680056 | solution.py:146
  117.9 4.0 fusion.77
  134.0 3.1 fusion.81
  149.8 4.0 fusion.77
  161.9 1.8 fusion.80
  165.9 3.1 fusion.81
  169.9 7.5 broadcast_in_dim.21
  177.4 136.3 %while.44 = (s32[]{:T(128)}, f32[512,2,2048]{2,1,0:T(2,128)}, f32[2,6]{0,1:T(8,128)S(1)}, s32[]{:T(128)}, s32[6]{0:T(128)S(1)}, /*index=5*/s32[6]{0:T(128)S(1)},...) while((s32[]{:T(128)}, f32[512,2,2048]{2,1,0:T(2,128)}, ...), condition=%wide.region_13.14_spmd, body=%wide.region_9.13_spmd.sunk | while | flops 3019835 | bytes 15514405 | solution.py:163
  189.1 3.0 fusion.84
  195.6 2.2 add_add_fusion.2
  197.8 47.5 %dynamic_update_slice.14 = f32[512,2,2048]{2,1,0:T(2,128)} dynamic-update-slice(f32[512,2,2048]{2,1,0:T(2,128)} %get-tuple-element.846, f32[257,2,257]{2,1,0:T(2,128)S(1)} %add_add_fusion.2, s32[]{:T(128)S(6)} %select_n.184, s32[]{:T(128)} %constant.305.clone.1..sunk.2, s32[]{:T(128)S(6)} %select_n.185) | dynamic-update-slice | bytes 1056788 | tf_op jit(solution)/shard_map/while/body/dynamic_update_slice | solution.py:155
  257.0 3.0 fusion.84
  263.5 2.2 add_add_fusion.2
  265.7 47.5 %dynamic_update_slice.14 = f32[512,2,2048]{2,1,0:T(2,128)} dynamic-update-slice(f32[512,2,2048]{2,1,0:T(2,128)} %get-tuple-element.846, f32[257,2,257]{2,1,0:T(2,128)S(1)} %add_add_fusion.2, s32[]{:T(128)S(6)} %select_n.184, s32[]{:T(128)} %constant.305.clone.1..sunk.2, s32[]{:T(128)S(6)} %select_n.185) | dynamic-update-slice | bytes 1056788 | tf_op jit(solution)/shard_map/while/body/dynamic_update_slice | solution.py:155
  313.8 6.3 slice.174
  320.1 3.1 collective-permute-start.1
  323.1 2.9 copy.50
  326.8 44.3 %collective-permute-done.1 = f32[256,2,2048]{2,1,0:T(2,128)} collective-permute-done((f32[256,2,2048]{2,1,0:T(2,128)}, f32[256,2,2048]{2,1,0:T(2,128)}, u32[]{:S(2)}, u32[]{:S(2)}) %collective-permute-start.1) | collective-permute-done | bytes 4194336 | tf_op jit(solution)/shard_map/ppermute | solution.py:12
  371.1 9.5 %slice_add_fusion = f32[256,2,2048]{2,1,0:T(2,128)} fusion(f32[256,2,2048]{2,1,0:T(2,128)} %collective-permute-done.1, f32[512,2,2048]{2,1,0:T(2,128)} %get-tuple-element.358), kind=kLoop, calls=%fused_computation.73 | loop fusion | flops 1048576 | bytes 12582912 | tf_op jit(solution)/shard_map/add | solution.py:166
  380.6 445.2 %all-reduce.8.cloned.1.call-done = f32[4,256,2,256]{3,2,1,0:T(2,128)} async-done(((f32[4,256,2,256]{3,2,1,0:T(2,128)}), f32[4,256,2,256]{3,2,1,0:T(2,128)}) %all-reduce.8.cloned.1.call-update) | async-done | bytes 2097168 | tf_op jit(solution)/shard_map/psum | solution.py:147
  825.7 3.6 copy.102
  (162 shorter events, 77.2 us)
Async XLA Ops:
  7.2 818.6 %all-reduce.8.cloned.1.call-start = ((), (), s32[]{:S(2)}) async-start(), calls=%async_computation | async-start | bytes 4194304 | tf_op jit(solution)/shard_map/psum | solution.py:147
  7.2 26.6 %collective-permute-start = (bf16[256,2,2048]{2,1,0:T(2,128)(2,1)}, bf16[256,2,2048]{2,1,0:T(2,128)(2,1)}, u32[]{:S(2)}, u32[]{:S(2)}) collective-permute-start(bf16[256,2,2048]{2,1,0:T(2,128)(2,1)} %param.21), channel_id=1, source_target_pairs={{1,0},{2,1},{3,2},{4,3},{5,4},{6,5},{7,6},{8,7},{9,8},{10,9},{11,1... | collective-permute-start | bytes 6291464 | tf_op jit(solution)/shard_map/ppermute | solution.py:12
  19.6 23.8 %copy-start.11 = (s32[6]{0:T(128)S(1)}, s32[6]{0:T(128)}, u32[]{:S(2)}) copy-start(s32[6]{0:T(128)} %param.24) | copy-start | bytes 76
  19.6 23.8 %copy-start.12 = (s32[6]{0:T(128)S(1)}, s32[6]{0:T(128)}, u32[]{:S(2)}) copy-start(s32[6]{0:T(128)} %param.25) | copy-start | bytes 76
  101.6 3.7 copy-start.10
  101.6 3.7 copy-start.13
  105.9 6.5 copy-start.6
  105.9 8.9 %copy-start.8 = (bf16[512,512]{1,0:T(8,128)(2,1)}, bf16[512,512]{1,0:T(8,128)(2,1)S(1)}, u32[]{:S(2)}) copy-start(bf16[512,512]{1,0:T(8,128)(2,1)S(1)} %get-tuple-element.804) | copy-start | bytes 1572868 | tf_op jit(solution)/shard_map/while
  112.8 0.7 copy-start.4
  123.9 1.6 copy-start
  130.0 1.8 copy-start.5
  131.9 1.6 copy-start.1
  133.5 3.7 copy-start.7
  133.5 3.7 copy-start.9
  134.0 3.2 copy-start.2
  137.8 6.5 copy-start.6
  137.8 8.9 %copy-start.8 = (bf16[512,512]{1,0:T(8,128)(2,1)}, bf16[512,512]{1,0:T(8,128)(2,1)S(1)}, u32[]{:S(2)}) copy-start(bf16[512,512]{1,0:T(8,128)(2,1)S(1)} %get-tuple-element.804) | copy-start | bytes 1572868 | tf_op jit(solution)/shard_map/while
  144.7 0.7 copy-start.4
  155.8 1.6 copy-start
  161.9 1.8 copy-start.5
  163.8 1.6 copy-start.1
  165.4 3.7 copy-start.7
  165.4 3.7 copy-start.9
  165.9 3.2 copy-start.2
  313.8 9.3 %copy-start.3 = (f32[4,256,2,256]{3,1,2,0:T(8,128)S(1)}, f32[4,256,2,256]{3,1,2,0:T(8,128)}, u32[]{:S(2)}) copy-start(f32[4,256,2,256]{3,1,2,0:T(8,128)} %get-tuple-element.359) | copy-start | bytes 6291460
  320.1 51.0 %collective-permute-start.1 = (f32[256,2,2048]{2,1,0:T(2,128)}, f32[256,2,2048]{2,1,0:T(2,128)}, u32[]{:S(2)}, u32[]{:S(2)}) collective-permute-start(f32[256,2,2048]{2,1,0:T(2,128)} %slice.174), channel_id=1, source_target_pairs={{0,1},{1,2},{2,3},{3,4},{4,5},{5,6},{6,7},{7,8},{8,9},{9,10},{10,1... | collective-permute-start | bytes 12582920 | tf_op jit(solution)/shard_map/ppermute | solution.py:12
Sparse Core Ops, SparseCore 0:
  326.2 499.4 all-reduce.7
where the time goes:
time: 853 us; the launch traced here: 837 us
  waiting for transfers between devices  504 us (59%)
  local copies, waits for them, and re-layouts  181 us (21%)
  other arithmetic  57.7 us (7%)
  loops' own time  55 us (6%)
  matrix products  18.5 us (2%)
  between operations  14.7 us (2%)
    psum x1, waiting for transfers between devices, shards(): probe_grad = lax.psum(probe_acc, 'row')  445 us
    dynamic_update_slice x2, local copies, waits for them, and re-layouts, settle(): lax.dynamic_update_slice(grad_ext, region + spread(obj_grad, frac_y, frac...  95 us
    ppermute x2, waiting for transfers between devices, passed_along(): return lax.ppermute(x, axis, pairs)  58.5 us
    another operation x1, loops' own time, shards(): windows = lax.map(cut, slot_ids)  30.5 us
  transfers between devices with their start and end apart: 3, of which 3 were waited for; matrix products, arithmetic and copies ran while one was open for 3% of the time, Pallas kernels for 0%

commit v1 on v0

v1 whole, which is shorter than its diff:
```python
import functools
import math

import jax
import jax.numpy as jnp
import ml_dtypes
import numpy as np
from jax import lax
from jax.experimental import pallas as pl
from jax.experimental.pallas import tpu as pltpu
from jax.sharding import PartitionSpec as P

F32 = jnp.float32
BF16 = jnp.bfloat16
LANES = 128
VMEM_BYTES = 56 * 2**20


def dft_tables(size):
    half = size // 2
    index = np.arange(size)
    angle = (index[:, None] * index[None, :] % size) * (2.0 * math.pi / size)
    scale = 1.0 / math.sqrt(size)
    cosine = (np.cos(angle) * scale).astype(ml_dtypes.bfloat16)
    sine = (np.sin(angle) * scale).astype(ml_dtypes.bfloat16)
    tables = []
    for parity in (0, 1):
        c, s = cosine[:half, parity::2], sine[:half, parity::2]
        tables.append(np.block([[c, -s], [s, c]]))
    order = np.zeros((size, size), ml_dtypes.bfloat16)
    order[2 * index[:half], index[:half]] = 1
    order[2 * index[:half] + 1, half + index[:half]] = 1
    even, odd = tables
    return tuple(jnp.asarray(t) for t in (even, odd, even.T.copy(), odd.T.copy(), order, order.T.copy()))


def dot(left, right):
    return jnp.dot(left, right, preferred_element_type=F32)


def fractions(code):
    return (code // 4).astype(F32) * 0.25, (code % 4).astype(F32) * 0.25


def project_kernel(
    slots, size, width, places, own, rim, probe, measured, even, odd, even_t, odd_t, order, order_t,
    grads, probe_acc, moved,
    cells, mixed, patch, folded, half_u, half_v, far, power, error, back, patch_grad, sems,
):
    half = size // 2
    modes = probe.shape[0]
    rows = own.shape[0]
    copies = [
        pltpu.make_async_copy(own, cells.at[pl.ds(0, rows)], sems.at[0]),
        pltpu.make_async_copy(rim, cells.at[pl.ds(rows, size)], sems.at[1]),
    ]
    for copy in copies:
        copy.start()
    probe_acc[...] = jnp.zeros_like(probe_acc)
    cells[rows + size :] = jnp.zeros((cells.shape[0] - rows - size, cells.shape[1]), BF16)
    for slot in range(slots):
        moved[0, slot] = 0.0
        moved[1, slot] = 0.0
    for copy in copies:
        copy.wait()
    span = mixed.shape[1]
    reach = size + LANES
    block = 32

    def one_slot(slot, _):
        top = places[0, slot]
        left = places[1, slot]
        frac_y, frac_x = fractions(places[2, slot])
        row0 = pl.multiple_of((top // 16) * 16, 16)
        col0 = pl.multiple_of((left // LANES) * LANES, LANES)
        down = top - row0
        across = left - col0
        source = lax.broadcasted_iota(jnp.int32, (reach, size), 0)
        target = lax.broadcasted_iota(jnp.int32, (reach, size), 1) + across
        here = (source == target).astype(F32)
        after = (source == target + 1).astype(F32)
        blend = jnp.concatenate([(1.0 - frac_x) * here + frac_x * after, after - here], axis=1).astype(BF16)
        source = lax.broadcasted_iota(jnp.int32, (span, size + 32), 1)
        target = lax.broadcasted_iota(jnp.int32, (span, size + 32), 0) + down
        lift = (source == target).astype(F32).astype(BF16)
        for part in range(2):
            start = pl.multiple_of(col0 + part * width, LANES)
            window = dot(lift, cells[pl.ds(row0, size + 32), pl.ds(start, reach)]).astype(BF16)
            mixed[part] = dot(window, blend)
        for part in range(2):
            for b in range(0, size, block):
                upper = mixed[part, pl.ds(b, block), :size]
                lower = mixed[part, pl.ds(b + 1, block), :size]
                patch[pl.ds(b, block), part * size : (part + 1) * size] = (1.0 - frac_y) * upper + frac_y * lower

        power[...] = jnp.zeros_like(power)

        def forward(mode, _):
            for b in range(0, size, block):
                at = pl.ds(b, block)
                preal, pimag = probe[mode, at, :size], probe[mode, at, size:]
                oreal, oimag = patch[at, :size], patch[at, size:]
                wreal = preal * oreal - pimag * oimag
                wimag = preal * oimag + pimag * oreal
                for part, wave in enumerate((wreal, wimag)):
                    folded[at, part * half : (part + 1) * half] = (wave[:, :half] + wave[:, half:]).astype(BF16)
                    folded[at, size + part * half : size + (part + 1) * half] = (wave[:, :half] - wave[:, half:]).astype(BF16)
            step = 64
            for b in range(0, half, step):
                for k, table in enumerate((even, odd)):
                    upper = dot(folded[b : b + step, k * size : (k + 1) * size], table[...])
                    lower = dot(folded[half + b : half + b + step, k * size : (k + 1) * size], table[...])
                    plus, minus = (upper + lower).astype(BF16), (upper - lower).astype(BF16)
                    for part in range(2):
                        to = slice(part * half + b, part * half + b + step)
                        cols = slice(part * half, (part + 1) * half)
                        half_u[to, k * half : (k + 1) * half] = plus[:, cols]
                        half_v[to, k * half : (k + 1) * half] = minus[:, cols]
            for k, (table, data) in enumerate(((even_t, half_u), (odd_t, half_v))):
                for c in range(0, size, half):
                    out = dot(table[...], data[:, c : c + half])
                    far[mode, k, :, c : c + half] = out
                    power[k * half : (k + 1) * half, c : c + half] += out[:half] * out[:half] + out[half:] * out[half:]
            return 0

        lax.fori_loop(0, modes, forward, 0)

        amplitude = dot(dot(order_t[...], measured[slot]).astype(BF16), order[...])
        power[...] = 1.0 - amplitude / jnp.maximum(jnp.sqrt(power[...]), 0.5)
        patch_grad[...] = jnp.zeros_like(patch_grad)

        def backward(mode, _):
            for k in range(2):
                for b in range(0, half, block):
                    ratio = power[k * half + b : k * half + b + block, :]
                    for part in range(2):
                        at = slice(part * half + b, part * half + b + block)
                        error[k, at, :] = (far[mode, k, at, :] * ratio).astype(BF16)
            for c in range(2):
                cols = slice(c * half, (c + 1) * half)
                first = dot(even[...], error[0, :, cols])
                second = dot(odd[...], error[1, :, cols])
                plus, minus = (first + second).astype(BF16), (first - second).astype(BF16)
                for part in range(2):
                    to = slice(c * size + part * half, c * size + (part + 1) * half)
                    back[:half, to] = plus[part * half : (part + 1) * half]
                    back[half:, to] = minus[part * half : (part + 1) * half]
            for b in range(0, size, block):
                at = pl.ds(b, block)
                first = dot(back[at, :size], even_t[...])
                second = dot(back[at, size:], odd_t[...])
                plus, minus = first + second, first - second
                for h, piece in enumerate((plus, minus)):
                    ureal, uimag = piece[:, :half], piece[:, half:]
                    re = slice(h * half, (h + 1) * half)
                    im = slice(size + h * half, size + (h + 1) * half)
                    preal, pimag = probe[mode, at, re], probe[mode, at, im]
                    oreal, oimag = patch[at, re], patch[at, im]
                    patch_grad[at, re] += preal * ureal + pimag * uimag
                    patch_grad[at, im] += preal * uimag - pimag * ureal
                    probe_acc[mode, at, re] += oreal * ureal + oimag * uimag
                    probe_acc[mode, at, im] += oreal * uimag - oimag * ureal
            return 0

        lax.fori_loop(0, modes, backward, 0)
        grads[slot] = patch_grad[...].astype(BF16)
        total_y = jnp.zeros((block, size), F32)
        total_x = jnp.zeros((block, size), F32)
        for part in range(2):
            for b in range(0, size, block):
                upper = mixed[part, pl.ds(b, block), :]
                lower = mixed[part, pl.ds(b + 1, block), :]
                grad = patch_grad[pl.ds(b, block), part * size : (part + 1) * size]
                total_y += grad * (lower[:, :size] - upper[:, :size])
                total_x += grad * ((1.0 - frac_y) * upper[:, size:] + frac_y * lower[:, size:])
        moved[0, slot] = jnp.sum(total_y) / size
        moved[1, slot] = jnp.sum(total_x) / size
        return 0

    lax.fori_loop(0, places[3, 0], one_slot, 0)


def project(places, own, rim, probe, measured, tables, width):
    slots, size, _ = measured.shape
    modes = probe.shape[0]
    span = size + 16
    reach = size + LANES
    vmem = pl.BlockSpec(memory_space=pltpu.VMEM)
    smem = pl.BlockSpec(memory_space=pltpu.SMEM)
    hbm = pl.BlockSpec(memory_space=pl.ANY)
    return pl.pallas_call(
        functools.partial(project_kernel, slots, size, width),
        in_specs=[smem, hbm, hbm] + [vmem] * 8,
        out_specs=[vmem, vmem, smem],
        out_shape=[
            jax.ShapeDtypeStruct((slots, size, 2 * size), BF16),
            jax.ShapeDtypeStruct(probe.shape, F32),
            jax.ShapeDtypeStruct((2, slots), F32),
        ],
        scratch_shapes=[
            pltpu.VMEM((own.shape[0] + size + 32, 2 * width), BF16),
            pltpu.VMEM((2, span, 2 * size), F32),
            pltpu.VMEM((size, 2 * size), F32),
            pltpu.VMEM((size, 2 * size), BF16),
            pltpu.VMEM((size, size), BF16),
            pltpu.VMEM((size, size), BF16),
            pltpu.VMEM((modes, 2, size, size), F32),
            pltpu.VMEM((size, size), F32),
            pltpu.VMEM((2, size, size), BF16),
            pltpu.VMEM((size, 2 * size), BF16),
            pltpu.VMEM((size, 2 * size), F32),
            pltpu.SemaphoreType.DMA((2,)),
        ],
        compiler_params=pltpu.CompilerParams(vmem_limit_bytes=VMEM_BYTES),
        name="project",
    )(places, own, rim, probe, measured, *tables)


def settle_kernel(size, width, places, grads, own, below, total):
    rows = own.shape[0]
    total[...] = jnp.zeros_like(total)
    reach = size + LANES
    span = size + 16

    def one_slot(slot, _):
        top = places[0, slot]
        left = places[1, slot]
        frac_y, frac_x = fractions(places[2, slot])
        row0 = pl.multiple_of((top // 8) * 8, 8)
        col0 = pl.multiple_of((left // LANES) * LANES, LANES)
        source = lax.broadcasted_iota(jnp.int32, (size, reach), 0) + (left - col0)
        target = lax.broadcasted_iota(jnp.int32, (size, reach), 1)
        along = jnp.where(source == target, 1.0 - frac_x, 0.0) + jnp.where(source + 1 == target, frac_x, 0.0)
        source = lax.broadcasted_iota(jnp.int32, (span, size), 1) + (top - row0)
        target = lax.broadcasted_iota(jnp.int32, (span, size), 0)
        down = jnp.where(source == target, 1.0 - frac_y, 0.0) + jnp.where(source + 1 == target, frac_y, 0.0)
        for part in range(2):
            wide = dot(grads[slot, :, part * size : (part + 1) * size], along.astype(BF16)).astype(BF16)
            start = pl.multiple_of(col0 + part * width, LANES)
            total[pl.ds(row0, span), pl.ds(start, reach)] += dot(down.astype(BF16), wide)
        return 0

    lax.fori_loop(0, places[3, 0], one_slot, 0)
    own[...] = total[:rows]
    below[...] = total[rows : rows + size].astype(BF16)


def settle(places, grads, rows, width):
    _, size, _ = grads.shape
    vmem = pl.BlockSpec(memory_space=pltpu.VMEM)
    smem = pl.BlockSpec(memory_space=pltpu.SMEM)
    return pl.pallas_call(
        functools.partial(settle_kernel, size, width),
        in_specs=[smem, vmem],
        out_specs=[vmem, vmem],
        out_shape=[
            jax.ShapeDtypeStruct((rows, 2 * width), F32),
            jax.ShapeDtypeStruct((size, 2 * width), BF16),
        ],
        scratch_shapes=[pltpu.VMEM((rows + size + 16, 2 * width), F32)],
        compiler_params=pltpu.CompilerParams(vmem_limit_bytes=VMEM_BYTES),
        name="settle",
    )(places, grads)


def passed_along(x, axis, by):
    length = lax.axis_size(axis)
    pairs = [(i, i + by) for i in range(length) if 0 <= i + by < length]
    return lax.ppermute(x, axis, pairs)


def summed(x, axis):
    length = lax.axis_size(axis)
    chips = length // 2
    me = lax.axis_index(axis)
    chip, core = me // 2, me % 2
    across = [(i, i ^ 1) for i in range(length)]
    x = x.reshape((2, x.shape[0] // 2) + x.shape[1:])
    mine = lax.dynamic_index_in_dim(x, core, 0, False)
    given = lax.dynamic_index_in_dim(x, 1 - core, 0, False).astype(BF16)
    mine = mine + lax.ppermute(given, axis, across).astype(F32)
    parts = mine.astype(BF16).reshape((chips, mine.shape[0] // chips) + mine.shape[1:])

    def ring(shift):
        return [(i, (i + 2 * shift) % length) for i in range(length)]

    got = [
        lax.ppermute(lax.dynamic_index_in_dim(parts, (chip + s) % chips, 0, False), axis, ring(s)) for s in range(1, chips)
    ]
    total = lax.dynamic_index_in_dim(mine.reshape(parts.shape), chip, 0, False)
    for piece in got:
        total = total + piece.astype(F32)
    total = total.astype(BF16)
    held = [total] + [lax.ppermute(total, axis, ring(s)) for s in range(1, chips)]
    whole = jnp.concatenate(held[::-1], axis=0)
    whole = jnp.concatenate([whole, whole], axis=0)
    size = total.shape[0]
    whole = lax.dynamic_slice_in_dim(whole, (chips - 1 - chip) * size, chips * size, 0)
    other = lax.ppermute(whole, axis, across)
    first = jnp.where(core == 0, whole, other)
    second = jnp.where(core == 0, other, whole)
    return jnp.concatenate([first, second], axis=0).astype(F32)


def shards(object_tiles, probe, measured, offset_row, offset_col, subpixel, live_count):
    rows, _, width = object_tiles.shape
    modes, size = probe.shape[:2]
    tables = dft_tables(size)
    rim = passed_along(object_tiles[:size], "row", -1)
    places = jnp.stack([offset_row, offset_col, subpixel, jnp.broadcast_to(live_count, offset_row.shape)])
    probe_flat = probe.reshape(modes, size, 2 * size)
    grads, probe_acc, moved = project(
        places, object_tiles.reshape(rows, 2 * width), rim.reshape(size, 2 * width), probe_flat, measured, tables, width
    )
    own, below = settle(places, grads, rows, width)
    below = passed_along(below, "row", 1)
    probe_grad = summed(probe_acc.reshape(modes * size, 2 * size), "row").reshape(probe.shape)
    object_grad = own.at[:size].add(below.astype(F32)).reshape(rows, 2, width)
    return object_grad, probe_grad, moved


def solution(mesh):
    in_specs = (
        P(("groups", "row"), None, None),
        P(),
        P(("groups", "row"), None, None),
        P(("groups", "row")),
        P(("groups", "row")),
        P(("groups", "row")),
        P(("groups", "row")),
    )
    out_specs = (
        P(("groups", "row"), None, None),
        P("groups", None, None, None),
        P(None, ("groups", "row")),
    )
    return jax.shard_map(shards, mesh=mesh, in_specs=in_specs, out_specs=out_specs, check_vma=False)
```

time: 853 us -> 173 us (0.20); the launches traced: 837 us -> 170 us
  waiting for transfers between devices: 504 us -> 37.6 us
  local copies, waits for them, and re-layouts: 181 us -> 20.5 us
  loops' own time: 55 us -> 0 us
  Pallas kernels: 0 us -> 50.7 us
  other arithmetic: 57.7 us -> 8.17 us
  starting transfers between devices: 5.82 us -> 51.4 us
  matrix products: 18.5 us -> 0 us
  between operations: 14.7 us -> 1.72 us
    psum x1 -> x0, waiting for transfers between devices: 445 us -> none  [shards(): probe_grad = lax.psum(probe_acc, 'row')]
    dynamic_update_slice x8 -> x0, local copies, waits for them, and re-layouts: 111 us -> none  [the longest x2 95 us: settle(): lax.dynamic_update_slice(grad_ext, region + spread(obj_grad, frac_y, frac...]
    another operation x3 -> x0, loops' own time: 55 us -> none  [the longest x1 30.5 us: shards(): windows = lax.map(cut, slot_ids)]
    pallas_call x0 -> x2, Pallas kernels: none -> 50.7 us  [the longest x1 41.9 us: project(): pl.pallas_call(functools.partial(project_kernel, slots, size, width), in_...]
    ppermute x0 -> x16, starting transfers between devices: none -> 46.7 us  [the longest x1 18.5 us: summed(): other = lax.ppermute(whole, axis, across)]
    ppermute x2, waiting for transfers between devices: 58.5 us -> 16.2 us  [passed_along(): return lax.ppermute(x, axis, pairs)]
    ppermute x0 -> x16, waiting for transfers between devices: none -> 21.4 us  [the longest x7 11.8 us: summed(): lax.ppermute(total, axis, ring(s))]
    dynamic_slice x32 -> x1, local copies, waits for them, and re-layouts: 19.9 us -> 0.04 us  [summed(): lax.dynamic_slice_in_dim(whole, (chips - 1 - chip) * size, chips * size, 0)]
  transfers between devices with their start and end apart: 3 -> 18, of which waited for: 3 -> 9; matrix products, arithmetic and copies ran while one was open for 3% -> 6% of each run, Pallas kernels for 0% -> 5%
where the time goes in v1:
time: 173 us; the launch traced here: 170 us
  starting transfers between devices  51.4 us (30%)
  Pallas kernels  50.7 us (29%)
  waiting for transfers between devices  37.6 us (22%)
  local copies, waits for them, and re-layouts  20.5 us (12%)
  other arithmetic  8.17 us (5%)
    pallas_call x1, Pallas kernels, project(): pl.pallas_call(functools.partial(project_kernel, slots, size, width), in_...  41.9 us
    ppermute x1, starting transfers between devices, summed(): other = lax.ppermute(whole, axis, across)  18.5 us
    ppermute x7, starting transfers between devices, summed(): lax.ppermute(lax.dynamic_index_in_dim(parts, (chip + s) % chips, 0, False...  17.6 us
    ppermute x2, waiting for transfers between devices, passed_along(): return lax.ppermute(x, axis, pairs)  16.2 us
    ppermute x7, waiting for transfers between devices, summed(): lax.ppermute(total, axis, ring(s))  11.8 us
    ppermute x7, starting transfers between devices, summed(): lax.ppermute(total, axis, ring(s))  10.6 us
    pallas_call x1, Pallas kernels, settle(): pl.pallas_call(functools.partial(settle_kernel, size, width), in_specs=[s...  8.79 us
    reshape x1, local copies, waits for them, and re-layouts, shards(): object_grad = own.at[:size].add(below.astype(F32)).reshape(rows, 2, width)  6.57 us
  transfers between devices with their start and end apart: 18, of which 9 were waited for; matrix products, arithmetic and copies ran while one was open for 6% of the time, Pallas kernels for 5%

profile of v1, /device:TPU:16, one launch (start us, length us, event | category | flops | bytes accessed | tf_op | source)
XLA Modules:
  0.0 170.1 jit_solution(16897376628682276423)
XLA Ops:
  0.6 2.7 %collective-permute-start = (bf16[256,2,2048]{2,1,0:T(2,128)(2,1)}, bf16[256,2,2048]{2,1,0:T(2,128)(2,1)}, u32[]{:S(2)}, u32[]{:S(2)}) collective-permute-start(bf16[256,2,2048]{2,1,0:T(2,128)(2,1)} %param.17), channel_id=1, source_target_pairs={{1,0},{2,1},{3,2},{4,3},{5,4},{6,5},{7,6},{8,7},{9,8},{10,9},{11,1... | collective-permute-start | bytes 6291464 | tf_op jit(solution)/shard_map/ppermute | solution.py:269
  4.1 4.0 %reshape.59.probe = f32[4,256,512]{2,1,0:T(8,128)} reshape(f32[4,256,2,256]{3,2,1,0:T(2,128)} %param.18) | data formatting | bytes 4194304 | tf_op jit(solution)/shard_map/reshape | solution.py:311
  8.2 2.2 %copy.16 = bf16[32,8,2,2048]{3,1,2,0:T(8,128)(2,1)} copy(bf16[32,8,2,2048]{3,2,1,0:T(2,128)(2,1)S(1)} %bitcast.48) | data formatting | bytes 4194304
  10.4 0.7 add_add_fusion.places
  11.0 16.2 %collective-permute-done = bf16[256,2,2048]{2,1,0:T(2,128)(2,1)} collective-permute-done((bf16[256,2,2048]{2,1,0:T(2,128)(2,1)}, bf16[256,2,2048]{2,1,0:T(2,128)(2,1)}, u32[]{:S(2)}, u32[]{:S(2)}) %collective-permute-start) | collective-permute-done | bytes 2097184 | tf_op jit(solution)/shard_map/ppermute | solution.py:269
  27.2 3.8 %copy.17 = bf16[32,8,2,2048]{3,1,2,0:T(8,128)(2,1)} copy(bf16[32,8,2,2048]{3,2,1,0:T(2,128)(2,1)} %bitcast.19) | data formatting | bytes 4194304
  31.0 41.9 %project.1 = (bf16[6,256,512]{2,1,0:T(8,128)(2,1)}, f32[4,256,512]{2,1,0:T(8,128)}, f32[2,6]{1,0:T(2,128)}) custom-call(s32[4,6]{1,0:T(4,128)} %add_add_fusion.places, bf16[256,4096]{1,0:T(8,128)(2,1)} %bitcast.46, bf16[256,4096]{1,0:T(8,128)(2,1)} %bitcast.47, f32[4,256,512]{2,1,0:T(8,128)} %reshape.59.probe, bf16[6,256,256]{2,1,0:T(8,128)(2,1)} %measured.1, ...), custom_call_target="tpu_custom_call" | custom-call | tf_op jit(solution)/shard_map/project/pallas_call | solution.py:191
  72.9 1.3 fusion
  74.4 1.7 %collective-permute-done.2 = bf16[512,512]{1,0:T(8,128)(2,1)S(1)} collective-permute-done((bf16[512,512]{1,0:T(8,128)(2,1)S(1)}, bf16[512,512]{1,0:T(8,128)(2,1)S(1)}, u32[]{:S(2)}, u32[]{:S(2)}) %collective-permute-start.2) | collective-permute-done | bytes 524320 | tf_op jit(solution)/shard_map/ppermute | solution.py:281
  76.2 1.4 fusion.8
  77.7 2.9 %collective-permute-start.9 = (bf16[64,512]{1,0:T(8,128)(2,1)S(1)}, bf16[64,512]{1,0:T(8,128)(2,1)S(1)}, u32[]{:S(2)}, u32[]{:S(2)}) collective-permute-start(bf16[64,512]{1,0:T(8,128)(2,1)S(1)} %get-tuple-element.38), channel_id=1, source_target_pairs={{0,14},{1,15},{2,0},{3,1},{4,2},{5,3},{6,4},{7,5},{8,6},{9,7},{10,... | collective-permute-start | bytes 196616 | tf_op jit(solution)/shard_map/ppermute | solution.py:288
  80.6 5.3 %collective-permute-start.8 = (bf16[64,512]{1,0:T(8,128)(2,1)S(1)}, bf16[64,512]{1,0:T(8,128)(2,1)S(1)}, u32[]{:S(2)}, u32[]{:S(2)}) collective-permute-start(bf16[64,512]{1,0:T(8,128)(2,1)S(1)} %get-tuple-element.39), channel_id=1, source_target_pairs={{0,12},{1,13},{2,14},{3,15},{4,0},{5,1},{6,2},{7,3},{8,4},{9,5},{1... | collective-permute-start | bytes 196616 | tf_op jit(solution)/shard_map/ppermute | solution.py:288
  85.9 5.0 %collective-permute-start.7 = (bf16[64,512]{1,0:T(8,128)(2,1)S(1)}, bf16[64,512]{1,0:T(8,128)(2,1)S(1)}, u32[]{:S(2)}, u32[]{:S(2)}) collective-permute-start(bf16[64,512]{1,0:T(8,128)(2,1)S(1)} %get-tuple-element.40), channel_id=1, source_target_pairs={{0,10},{1,11},{2,12},{3,13},{4,14},{5,15},{6,0},{7,1},{8,2},{9,3},... | collective-permute-start | bytes 196616 | tf_op jit(solution)/shard_map/ppermute | solution.py:288
  91.0 1.4 collective-permute-start.6
  92.3 2.9 %collective-permute-start.5 = (bf16[64,512]{1,0:T(8,128)(2,1)S(1)}, bf16[64,512]{1,0:T(8,128)(2,1)S(1)}, u32[]{:S(2)}, u32[]{:S(2)}) collective-permute-start(bf16[64,512]{1,0:T(8,128)(2,1)S(1)} %get-tuple-element.42), channel_id=1, source_target_pairs={{0,6},{1,7},{2,8},{3,9},{4,10},{5,11},{6,12},{7,13},{8,14},{9,15},... | collective-permute-start | bytes 196616 | tf_op jit(solution)/shard_map/ppermute | solution.py:288
  95.3 3.5 %collective-permute-done.7 = bf16[64,512]{1,0:T(8,128)(2,1)S(1)} collective-permute-done((bf16[64,512]{1,0:T(8,128)(2,1)S(1)}, bf16[64,512]{1,0:T(8,128)(2,1)S(1)}, u32[]{:S(2)}, u32[]{:S(2)}) %collective-permute-start.7) | collective-permute-done | bytes 65568 | tf_op jit(solution)/shard_map/ppermute | solution.py:288
  98.8 0.7 collective-permute-done.6
  99.5 2.2 %collective-permute-done.4 = bf16[64,512]{1,0:T(8,128)(2,1)S(1)} collective-permute-done((bf16[64,512]{1,0:T(8,128)(2,1)S(1)}, bf16[64,512]{1,0:T(8,128)(2,1)S(1)}, u32[]{:S(2)}, u32[]{:S(2)}) %collective-permute-start.4) | collective-permute-done | bytes 65568 | tf_op jit(solution)/shard_map/ppermute | solution.py:288
  101.8 8.8 %settle.1 = (f32[256,4096]{1,0:T(8,128)}, bf16[256,4096]{1,0:T(8,128)(2,1)}) custom-call(s32[4,6]{1,0:T(4,128)} %add_add_fusion.places, bf16[6,256,512]{2,1,0:T(8,128)(2,1)} %get-tuple-element.28.grads), custom_call_target="tpu_custom_call" | custom-call | tf_op jit(solution)/shard_map/settle/pallas_call | solution.py:252
  110.6 1.9 %collective-permute-start.1 = (bf16[256,4096]{1,0:T(8,128)(2,1)}, bf16[256,4096]{1,0:T(8,128)(2,1)}, u32[]{:S(2)}, u32[]{:S(2)}) collective-permute-start(bf16[256,4096]{1,0:T(8,128)(2,1)} %get-tuple-element.30), channel_id=1, source_target_pairs={{0,1},{1,2},{2,3},{3,4},{4,5},{5,6},{6,7},{7,8},{8,9},{9,10},{10,1... | collective-permute-start | bytes 6291464 | tf_op jit(solution)/shard_map/ppermute | solution.py:269
  112.5 3.3 %collective-permute-start.15 = (bf16[64,512]{1,0:T(8,128)(2,1)S(1)}, bf16[64,512]{1,0:T(8,128)(2,1)S(1)}, u32[]{:S(2)}, u32[]{:S(2)}) collective-permute-start(bf16[64,512]{1,0:T(8,128)(2,1)S(1)} %fusion.7), channel_id=1, source_target_pairs={{0,4},{1,5},{2,6},{3,7},{4,8},{5,9},{6,10},{7,11},{8,12},{9,13},{1... | collective-permute-start | bytes 196616 | tf_op jit(solution)/shard_map/ppermute | solution.py:294
  115.8 2.5 %collective-permute-start.14 = (bf16[64,512]{1,0:T(8,128)(2,1)S(1)}, bf16[64,512]{1,0:T(8,128)(2,1)S(1)}, u32[]{:S(2)}, u32[]{:S(2)}) collective-permute-start(bf16[64,512]{1,0:T(8,128)(2,1)S(1)} %fusion.7), channel_id=1, source_target_pairs={{0,6},{1,7},{2,8},{3,9},{4,10},{5,11},{6,12},{7,13},{8,14},{9,15},... | collective-permute-start | bytes 196616 | tf_op jit(solution)/shard_map/ppermute | solution.py:294
  118.4 5.4 %collective-permute-done.11 = bf16[64,512]{1,0:T(8,128)(2,1)S(1)} collective-permute-done((bf16[64,512]{1,0:T(8,128)(2,1)S(1)}, bf16[64,512]{1,0:T(8,128)(2,1)S(1)}, u32[]{:S(2)}, u32[]{:S(2)}) %collective-permute-start.11) | collective-permute-done | bytes 65568 | tf_op jit(solution)/shard_map/ppermute | solution.py:294
  123.8 2.7 %collective-permute-start.12 = (bf16[64,512]{1,0:T(8,128)(2,1)S(1)}, bf16[64,512]{1,0:T(8,128)(2,1)S(1)}, u32[]{:S(2)}, u32[]{:S(2)}) collective-permute-start(bf16[64,512]{1,0:T(8,128)(2,1)S(1)} %fusion.7), channel_id=1, source_target_pairs={{0,10},{1,11},{2,12},{3,13},{4,14},{5,15},{6,0},{7,1},{8,2},{9,3},... | collective-permute-start | bytes 196616 | tf_op jit(solution)/shard_map/ppermute | solution.py:294
  126.5 3.2 %collective-permute-done.12 = bf16[64,512]{1,0:T(8,128)(2,1)S(1)} collective-permute-done((bf16[64,512]{1,0:T(8,128)(2,1)S(1)}, bf16[64,512]{1,0:T(8,128)(2,1)S(1)}, u32[]{:S(2)}, u32[]{:S(2)}) %collective-permute-start.12) | collective-permute-done | bytes 65568 | tf_op jit(solution)/shard_map/ppermute | solution.py:294
  129.7 1.9 %collective-permute-start.13 = (bf16[64,512]{1,0:T(8,128)(2,1)S(1)}, bf16[64,512]{1,0:T(8,128)(2,1)S(1)}, u32[]{:S(2)}, u32[]{:S(2)}) collective-permute-start(bf16[64,512]{1,0:T(8,128)(2,1)S(1)} %fusion.7), channel_id=1, source_target_pairs={{0,8},{1,9},{2,10},{3,11},{4,12},{5,13},{6,14},{7,15},{8,0},{9,1},... | collective-permute-start | bytes 196616 | tf_op jit(solution)/shard_map/ppermute | solution.py:294
  131.6 3.2 %collective-permute-done.13 = bf16[64,512]{1,0:T(8,128)(2,1)S(1)} collective-permute-done((bf16[64,512]{1,0:T(8,128)(2,1)S(1)}, bf16[64,512]{1,0:T(8,128)(2,1)S(1)}, u32[]{:S(2)}, u32[]{:S(2)}) %collective-permute-start.13) | collective-permute-done | bytes 65568 | tf_op jit(solution)/shard_map/ppermute | solution.py:294
  135.1 18.5 %collective-permute-start.17 = (bf16[512,512]{1,0:T(8,128)(2,1)S(1)}, bf16[512,512]{1,0:T(8,128)(2,1)S(1)}, u32[]{:S(2)}, u32[]{:S(2)}) collective-permute-start(bf16[512,512]{1,0:T(8,128)(2,1)S(1)} %constant_dynamic-slice_fusion), channel_id=1, source_target_pairs={{0,1},{1,0},{2,3},{3,2},{4,5},{5,4},{6,7},{7,6},{8,9},{9,8},{10,11... | collective-permute-start | bytes 1572872 | tf_op jit(solution)/shard_map/ppermute | solution.py:299
  153.6 1.5 collective-permute-done.17
  155.7 2.4 %reshape.63 = f32[4,256,2,256]{3,2,1,0:T(2,128)} reshape(f32[1024,512]{1,0:T(8,128)S(1)} %maximum_convert_fusion) | data formatting | bytes 4194304 | tf_op jit(solution)/shard_map/convert_element_type | solution.py:302
  158.0 5.5 %convert_add_fusion = f32[256,4096]{1,0:T(8,128)} fusion(f32[256,4096]{1,0:T(8,128)} %get-tuple-element.29, bf16[256,4096]{1,0:T(8,128)(2,1)} %collective-permute-done.1), kind=kLoop, calls=%fused_computation | loop fusion | flops 2097152 | bytes 10485760 | tf_op jit(solution)/shard_map/add | solution.py:318
  163.5 6.6 %reshape.60 = f32[256,2,2048]{2,1,0:T(2,128)} reshape(f32[256,4096]{1,0:T(8,128)} %convert_add_fusion) | data formatting | bytes 8388608 | tf_op jit(solution)/shard_map/reshape | solution.py:318
  (45 shorter events, 1.1 us)
Async XLA Ops:
  0.6 26.6 %collective-permute-start = (bf16[256,2,2048]{2,1,0:T(2,128)(2,1)}, bf16[256,2,2048]{2,1,0:T(2,128)(2,1)}, u32[]{:S(2)}, u32[]{:S(2)}) collective-permute-start(bf16[256,2,2048]{2,1,0:T(2,128)(2,1)} %param.17), channel_id=1, source_target_pairs={{1,0},{2,1},{3,2},{4,3},{5,4},{6,5},{7,6},{8,7},{9,8},{10,9},{11,1... | collective-permute-start | bytes 6291464 | tf_op jit(solution)/shard_map/ppermute | solution.py:269
  4.1 4.0 %copy-start = (bf16[256,2,2048]{2,1,0:T(2,128)(2,1)S(1)}, bf16[256,2,2048]{2,1,0:T(2,128)(2,1)}, u32[]{:S(2)}) copy-start(bf16[256,2,2048]{2,1,0:T(2,128)(2,1)} %param.17) | copy-start | bytes 6291460
  8.1 2.2 %copy-start.1 = (s32[6]{0:T(128)S(1)}, s32[6]{0:T(128)}, u32[]{:S(2)}) copy-start(s32[6]{0:T(128)} %param.22) | copy-start | bytes 76
  8.1 2.2 %copy-start.2 = (s32[6]{0:T(128)S(1)}, s32[6]{0:T(128)}, u32[]{:S(2)}) copy-start(s32[6]{0:T(128)} %param.21) | copy-start | bytes 76
  8.1 2.2 %copy-start.3 = (s32[6]{0:T(128)S(1)}, s32[6]{0:T(128)}, u32[]{:S(2)}) copy-start(s32[6]{0:T(128)} %param.20) | copy-start | bytes 76
  74.2 2.0 %collective-permute-start.2 = (bf16[512,512]{1,0:T(8,128)(2,1)S(1)}, bf16[512,512]{1,0:T(8,128)(2,1)S(1)}, u32[]{:S(2)}, u32[]{:S(2)}) collective-permute-start(bf16[512,512]{1,0:T(8,128)(2,1)S(1)} %fusion), channel_id=1, source_target_pairs={{0,1},{1,0},{2,3},{3,2},{4,5},{5,4},{6,7},{7,6},{8,9},{9,8},{10,11... | collective-permute-start | bytes 1572872 | tf_op jit(solution)/shard_map/ppermute | solution.py:281
  77.6 14.7 %collective-permute-start.3 = (bf16[64,512]{1,0:T(8,128)(2,1)S(1)}, bf16[64,512]{1,0:T(8,128)(2,1)S(1)}, u32[]{:S(2)}, u32[]{:S(2)}) collective-permute-start(bf16[64,512]{1,0:T(8,128)(2,1)S(1)} %get-tuple-element.37), channel_id=1, source_target_pairs={{0,2},{1,3},{2,4},{3,5},{4,6},{5,7},{6,8},{7,9},{8,10},{9,11},{10,... | collective-permute-start | bytes 196616 | tf_op jit(solution)/shard_map/ppermute | solution.py:288
  77.7 17.5 %collective-permute-start.9 = (bf16[64,512]{1,0:T(8,128)(2,1)S(1)}, bf16[64,512]{1,0:T(8,128)(2,1)S(1)}, u32[]{:S(2)}, u32[]{:S(2)}) collective-permute-start(bf16[64,512]{1,0:T(8,128)(2,1)S(1)} %get-tuple-element.38), channel_id=1, source_target_pairs={{0,14},{1,15},{2,0},{3,1},{4,2},{5,3},{6,4},{7,5},{8,6},{9,7},{10,... | collective-permute-start | bytes 196616 | tf_op jit(solution)/shard_map/ppermute | solution.py:288
  80.6 14.6 %collective-permute-start.8 = (bf16[64,512]{1,0:T(8,128)(2,1)S(1)}, bf16[64,512]{1,0:T(8,128)(2,1)S(1)}, u32[]{:S(2)}, u32[]{:S(2)}) collective-permute-start(bf16[64,512]{1,0:T(8,128)(2,1)S(1)} %get-tuple-element.39), channel_id=1, source_target_pairs={{0,12},{1,13},{2,14},{3,15},{4,0},{5,1},{6,2},{7,3},{8,4},{9,5},{1... | collective-permute-start | bytes 196616 | tf_op jit(solution)/shard_map/ppermute | solution.py:288
  85.9 12.8 %collective-permute-start.7 = (bf16[64,512]{1,0:T(8,128)(2,1)S(1)}, bf16[64,512]{1,0:T(8,128)(2,1)S(1)}, u32[]{:S(2)}, u32[]{:S(2)}) collective-permute-start(bf16[64,512]{1,0:T(8,128)(2,1)S(1)} %get-tuple-element.40), channel_id=1, source_target_pairs={{0,10},{1,11},{2,12},{3,13},{4,14},{5,15},{6,0},{7,1},{8,2},{9,3},... | collective-permute-start | bytes 196616 | tf_op jit(solution)/shard_map/ppermute | solution.py:288
  91.0 8.5 %collective-permute-start.6 = (bf16[64,512]{1,0:T(8,128)(2,1)S(1)}, bf16[64,512]{1,0:T(8,128)(2,1)S(1)}, u32[]{:S(2)}, u32[]{:S(2)}) collective-permute-start(bf16[64,512]{1,0:T(8,128)(2,1)S(1)} %get-tuple-element.41), channel_id=1, source_target_pairs={{0,8},{1,9},{2,10},{3,11},{4,12},{5,13},{6,14},{7,15},{8,0},{9,1},... | collective-permute-start | bytes 196616 | tf_op jit(solution)/shard_map/ppermute | solution.py:288
  92.3 7.1 %collective-permute-start.5 = (bf16[64,512]{1,0:T(8,128)(2,1)S(1)}, bf16[64,512]{1,0:T(8,128)(2,1)S(1)}, u32[]{:S(2)}, u32[]{:S(2)}) collective-permute-start(bf16[64,512]{1,0:T(8,128)(2,1)S(1)} %get-tuple-element.42), channel_id=1, source_target_pairs={{0,6},{1,7},{2,8},{3,9},{4,10},{5,11},{6,12},{7,13},{8,14},{9,15},... | collective-permute-start | bytes 196616 | tf_op jit(solution)/shard_map/ppermute | solution.py:288
  95.3 6.4 %collective-permute-start.4 = (bf16[64,512]{1,0:T(8,128)(2,1)S(1)}, bf16[64,512]{1,0:T(8,128)(2,1)S(1)}, u32[]{:S(2)}, u32[]{:S(2)}) collective-permute-start(bf16[64,512]{1,0:T(8,128)(2,1)S(1)} %get-tuple-element.43), channel_id=1, source_target_pairs={{0,4},{1,5},{2,6},{3,7},{4,8},{5,9},{6,10},{7,11},{8,12},{9,13},{1... | collective-permute-start | bytes 196616 | tf_op jit(solution)/shard_map/ppermute | solution.py:288
  101.7 16.7 %collective-permute-start.10 = (bf16[64,512]{1,0:T(8,128)(2,1)S(1)}, bf16[64,512]{1,0:T(8,128)(2,1)S(1)}, u32[]{:S(2)}, u32[]{:S(2)}) collective-permute-start(bf16[64,512]{1,0:T(8,128)(2,1)S(1)} %fusion.7), channel_id=1, source_target_pairs={{0,14},{1,15},{2,0},{3,1},{4,2},{5,3},{6,4},{7,5},{8,6},{9,7},{10,... | collective-permute-start | bytes 196616 | tf_op jit(solution)/shard_map/ppermute | solution.py:294
  110.6 47.4 %collective-permute-start.1 = (bf16[256,4096]{1,0:T(8,128)(2,1)}, bf16[256,4096]{1,0:T(8,128)(2,1)}, u32[]{:S(2)}, u32[]{:S(2)}) collective-permute-start(bf16[256,4096]{1,0:T(8,128)(2,1)} %get-tuple-element.30), channel_id=1, source_target_pairs={{0,1},{1,2},{2,3},{3,4},{4,5},{5,6},{6,7},{7,8},{8,9},{9,10},{10,1... | collective-permute-start | bytes 6291464 | tf_op jit(solution)/shard_map/ppermute | solution.py:269
  112.5 22.4 %collective-permute-start.16 = (bf16[64,512]{1,0:T(8,128)(2,1)S(1)}, bf16[64,512]{1,0:T(8,128)(2,1)S(1)}, u32[]{:S(2)}, u32[]{:S(2)}) collective-permute-start(bf16[64,512]{1,0:T(8,128)(2,1)S(1)} %fusion.7), channel_id=1, source_target_pairs={{0,2},{1,3},{2,4},{3,5},{4,6},{5,7},{6,8},{7,9},{8,10},{9,11},{10,... | collective-permute-start | bytes 196616 | tf_op jit(solution)/shard_map/ppermute | solution.py:294
  112.5 22.3 %collective-permute-start.15 = (bf16[64,512]{1,0:T(8,128)(2,1)S(1)}, bf16[64,512]{1,0:T(8,128)(2,1)S(1)}, u32[]{:S(2)}, u32[]{:S(2)}) collective-permute-start(bf16[64,512]{1,0:T(8,128)(2,1)S(1)} %fusion.7), channel_id=1, source_target_pairs={{0,4},{1,5},{2,6},{3,7},{4,8},{5,9},{6,10},{7,11},{8,12},{9,13},{1... | collective-permute-start | bytes 196616 | tf_op jit(solution)/shard_map/ppermute | solution.py:294
  115.8 19.0 %collective-permute-start.14 = (bf16[64,512]{1,0:T(8,128)(2,1)S(1)}, bf16[64,512]{1,0:T(8,128)(2,1)S(1)}, u32[]{:S(2)}, u32[]{:S(2)}) collective-permute-start(bf16[64,512]{1,0:T(8,128)(2,1)S(1)} %fusion.7), channel_id=1, source_target_pairs={{0,6},{1,7},{2,8},{3,9},{4,10},{5,11},{6,12},{7,13},{8,14},{9,15},... | collective-permute-start | bytes 196616 | tf_op jit(solution)/shard_map/ppermute | solution.py:294
  118.4 5.4 %collective-permute-start.11 = (bf16[64,512]{1,0:T(8,128)(2,1)S(1)}, bf16[64,512]{1,0:T(8,128)(2,1)S(1)}, u32[]{:S(2)}, u32[]{:S(2)}) collective-permute-start(bf16[64,512]{1,0:T(8,128)(2,1)S(1)} %fusion.7), channel_id=1, source_target_pairs={{0,12},{1,13},{2,14},{3,15},{4,0},{5,1},{6,2},{7,3},{8,4},{9,5},{1... | collective-permute-start | bytes 196616 | tf_op jit(solution)/shard_map/ppermute | solution.py:294
  123.8 5.9 %collective-permute-start.12 = (bf16[64,512]{1,0:T(8,128)(2,1)S(1)}, bf16[64,512]{1,0:T(8,128)(2,1)S(1)}, u32[]{:S(2)}, u32[]{:S(2)}) collective-permute-start(bf16[64,512]{1,0:T(8,128)(2,1)S(1)} %fusion.7), channel_id=1, source_target_pairs={{0,10},{1,11},{2,12},{3,13},{4,14},{5,15},{6,0},{7,1},{8,2},{9,3},... | collective-permute-start | bytes 196616 | tf_op jit(solution)/shard_map/ppermute | solution.py:294
  129.7 5.2 %collective-permute-start.13 = (bf16[64,512]{1,0:T(8,128)(2,1)S(1)}, bf16[64,512]{1,0:T(8,128)(2,1)S(1)}, u32[]{:S(2)}, u32[]{:S(2)}) collective-permute-start(bf16[64,512]{1,0:T(8,128)(2,1)S(1)} %fusion.7), channel_id=1, source_target_pairs={{0,8},{1,9},{2,10},{3,11},{4,12},{5,13},{6,14},{7,15},{8,0},{9,1},... | collective-permute-start | bytes 196616 | tf_op jit(solution)/shard_map/ppermute | solution.py:294
  135.1 20.0 %collective-permute-start.17 = (bf16[512,512]{1,0:T(8,128)(2,1)S(1)}, bf16[512,512]{1,0:T(8,128)(2,1)S(1)}, u32[]{:S(2)}, u32[]{:S(2)}) collective-permute-start(bf16[512,512]{1,0:T(8,128)(2,1)S(1)} %constant_dynamic-slice_fusion), channel_id=1, source_target_pairs={{0,1},{1,0},{2,3},{3,2},{4,5},{5,4},{6,7},{7,6},{8,9},{9,8},{10,11... | collective-permute-start | bytes 1572872 | tf_op jit(solution)/shard_map/ppermute | solution.py:299
